TPU v7x, 32 devices: a whole 2x2x4 slice. The times are simulated.
32 devices in a mesh: seq: 2 (over x), head: 4 (over z), dp: 4 (over y, core).
Axes of the slice: x: 2, y: 2, z: 4, core: 2. Of those that a mesh axis runs over, the one named last changes fastest.
Arguments:
- layer_input: bfloat16 [4, 1024, 2048], P('dp', 'seq'), may hold values from -6 to 6
- w_query: bfloat16 [2048, 2048], P(None, 'head'), may hold values from -0.125 to 0.125
- w_key: bfloat16 [2048, 2048], P(None, 'head'), may hold values from -0.125 to 0.125
- w_value: bfloat16 [2048, 2048], P(None, 'head'), may hold values from -0.125 to 0.125
- w_out: bfloat16 [2048, 2048], P('head'), may hold values from -0.125 to 0.125
- out_grad: bfloat16 [4, 1024, 2048], P('dp', 'seq'), may hold values from -6 to 6
Outputs:
- input_grad: bfloat16 [4, 1024, 2048], P('dp', 'seq', 'head')
- grad_query: float32 [2048, 2048], P(('seq', 'dp'), 'head')
- grad_key: float32 [2048, 2048], P(('seq', 'dp'), 'head')
- grad_value: float32 [2048, 2048], P(('seq', 'dp'), 'head')
- grad_out: float32 [2048, 2048], P('head', ('seq', 'dp'))
All inputs are finite; a program needn't handle non-finite values.
Results may differ from a plain program's by a relative error of at most 0.0073.
Values sent between devices are 32-bit elements; how exact they have to be, the bound alone decides.
No kernel may reach another device: no remote copies, remote signals or barrier semaphores. Data moves between devices by JAX's collectives and lax.ppermute only.
A program may use at most 128 MiB of HBM per device.

v0:
```python
import jax
import jax.numpy as jnp
from jax import lax
from jax.sharding import PartitionSpec as P

HEAD_DIM = 128


def entering(x, axis, combine, identity, reverse):
    peers, here = (lax.axis_size(axis), lax.axis_index(axis))
    everything = lax.all_gather(x, axis)
    start = jnp.broadcast_to(jnp.asarray(identity, x.dtype), x.shape)

    def step(k, before):
        at = peers - 1 - k if reverse else k
        reached = at > here if reverse else at < here
        new = combine(before, everything[at])
        return jnp.where(reached, new, before)

    return lax.fori_loop(0, peers, step, start)


def add_states(earlier, later_sum):
    return earlier + later_sum


def local(layer_input, w_query, w_key, w_value, w_out, out_grad):
    num_rows = layer_input.shape[1]
    local_heads = w_query.shape[1] // HEAD_DIM
    in_rows = layer_input[0]
    grad_rows = out_grad[0]

    def project(weight):
        result = jnp.dot(in_rows, weight, preferred_element_type=jnp.float32).astype(jnp.bfloat16)
        return result.reshape(num_rows, local_heads, HEAD_DIM)

    queries = project(w_query)
    key_rows = project(w_key)
    value_rows = project(w_value)
    row_start = lax.axis_index("seq") * num_rows
    positions = (row_start + jnp.arange(num_rows, dtype=jnp.int32)).astype(jnp.float32)
    pos_scale = 1.0 / jnp.sqrt(HEAD_DIM * (positions + 1.0))
    backward = jnp.einsum("td,kd->tk", grad_rows, w_out, preferred_element_type=jnp.float32)
    grad_in = (
        (backward * pos_scale[:, None])
        .astype(jnp.bfloat16)
        .reshape(num_rows, local_heads, HEAD_DIM)
    )
    kv_state = jnp.einsum("thd,the->hde", key_rows, value_rows, preferred_element_type=jnp.float32)
    qg_state = jnp.einsum("thd,the->hde", queries, grad_in, preferred_element_type=jnp.float32)
    zero_state = jnp.zeros_like(kv_state)
    prefix = entering(kv_state, "seq", add_states, zero_state, False)
    suffix = entering(qg_state, "seq", add_states, zero_state, True)
    prefix = prefix.astype(jnp.bfloat16)
    suffix = suffix.astype(jnp.bfloat16)
    causal = (jnp.arange(num_rows)[:, None] >= jnp.arange(num_rows)[None, :])[None]
    scores = jnp.einsum("thd,shd->hts", queries, key_rows, preferred_element_type=jnp.float32)
    scores_qk = jnp.where(causal, scores, 0.0).astype(jnp.bfloat16)
    scores_g = jnp.einsum("thd,shd->hts", grad_in, value_rows, preferred_element_type=jnp.float32)
    scores_gv = jnp.where(causal, scores_g, 0.0).astype(jnp.bfloat16)
    inner_sum = jnp.einsum(
        "hts,she->the", scores_qk, value_rows, preferred_element_type=jnp.float32
    )
    cross_sum = jnp.einsum("thd,hde->the", queries, prefix, preferred_element_type=jnp.float32)
    attention = (
        ((inner_sum + cross_sum) * pos_scale[:, None, None])
        .astype(jnp.bfloat16)
        .reshape(num_rows, local_heads * HEAD_DIM)
    )
    d_query = jnp.einsum("hts,shd->thd", scores_gv, key_rows, preferred_element_type=jnp.float32)
    d_query = d_query + jnp.einsum(
        "the,hde->thd", grad_in, prefix, preferred_element_type=jnp.float32
    )
    d_keys = jnp.einsum("hts,thd->shd", scores_gv, queries, preferred_element_type=jnp.float32)
    d_keys = d_keys + jnp.einsum(
        "she,hde->shd", value_rows, suffix, preferred_element_type=jnp.float32
    )
    d_values = jnp.einsum("hts,the->she", scores_qk, grad_in, preferred_element_type=jnp.float32)
    d_values = d_values + jnp.einsum(
        "shd,hde->she", key_rows, suffix, preferred_element_type=jnp.float32
    )
    d_query = d_query.astype(jnp.bfloat16).reshape(num_rows, local_heads * HEAD_DIM)
    d_keys = d_keys.astype(jnp.bfloat16).reshape(num_rows, local_heads * HEAD_DIM)
    d_values = d_values.astype(jnp.bfloat16).reshape(num_rows, local_heads * HEAD_DIM)
    head_terms = jnp.einsum("tk,dk->td", d_query, w_query, preferred_element_type=jnp.float32)
    head_terms = head_terms + jnp.einsum(
        "tk,dk->td", d_keys, w_key, preferred_element_type=jnp.float32
    )
    head_terms = head_terms + jnp.einsum(
        "tk,dk->td", d_values, w_value, preferred_element_type=jnp.float32
    )
    input_grad = lax.psum_scatter(head_terms, "head", scatter_dimension=1, tiled=True).astype(
        jnp.bfloat16
    )[None]
    total_rows = lax.axis_size("seq") * lax.axis_size("dp") * num_rows
    grad_scale = jnp.float32(1.0) / jnp.sqrt(jnp.float32(total_rows))
    term_query = (
        jnp.einsum("td,tk->dk", in_rows, d_query, preferred_element_type=jnp.float32) * grad_scale
    )
    term_key = (
        jnp.einsum("td,tk->dk", in_rows, d_keys, preferred_element_type=jnp.float32) * grad_scale
    )
    term_value = (
        jnp.einsum("td,tk->dk", in_rows, d_values, preferred_element_type=jnp.float32) * grad_scale
    )
    term_out = (
        jnp.einsum("td,tk->dk", grad_rows, attention, preferred_element_type=jnp.float32)
        * grad_scale
    )
    summed = (
        lax.psum_scatter(term_query, ("seq", "dp"), scatter_dimension=0, tiled=True),
        lax.psum_scatter(term_key, ("seq", "dp"), scatter_dimension=0, tiled=True),
        lax.psum_scatter(term_value, ("seq", "dp"), scatter_dimension=0, tiled=True),
        lax.psum_scatter(term_out, ("seq", "dp"), scatter_dimension=0, tiled=True),
    )
    return (input_grad, summed[0], summed[1], summed[2], summed[3].T)


def solution(mesh):
    return jax.shard_map(
        local,
        mesh=mesh,
        in_specs=(
            P("dp", "seq", None),
            P(None, "head"),
            P(None, "head"),
            P(None, "head"),
            P("head", None),
            P("dp", "seq", None),
        ),
        out_specs=(
            P("dp", "seq", "head"),
            P(("seq", "dp"), "head"),
            P(("seq", "dp"), "head"),
            P(("seq", "dp"), "head"),
            P("head", ("seq", "dp")),
        ),
        check_vma=False,
    )
```

profile of v0, /device:TPU:0, one launch (start us, length us, event | category | flops | bytes accessed | tf_op | source)
XLA Modules:
  0.0 337.2 jit_solution(9172116064104449764)
XLA Ops:
  7.2 0.8 iota_compare_fusion
  8.0 0.8 copy-done
  8.9 3.0 fusion.23
  11.9 1.3 fusion.29
  13.2 0.8 copy-done.7
  14.0 0.3 fusion.40
  14.3 9.9 %all-gather.1 = f32[8,128,128]{2,1,0:T(8,128)S(1)} all-gather(f32[4,128,128]{2,1,0:T(8,128)S(1)} %fusion.40), channel_id=3, replica_groups=mesh['seq'=2,'head'=4,'dp'=4] {'seq'}, dimensions={0}, use_global_device_ids=true | all-gather | bytes 786432 | tf_op jit(solution)/shard_map/all_gather | solution.py:11
  24.2 0.2 while.31
  24.3 0.1 add_select_fusion.5
  24.4 2.9 fusion.17
  27.4 0.8 select_convert_fusion
  28.2 0.4 copy-done.8
  28.6 0.4 fusion.42
  29.1 0.3 fusion.28
  29.4 0.5 copy-done.1
  30.0 3.2 multiply_bitcast_fusion.1
  33.2 2.9 fusion.20
  36.2 0.3 fusion.37
  36.5 8.3 %all-gather = f32[8,128,128]{2,1,0:T(8,128)S(1)} all-gather(f32[4,128,128]{2,1,0:T(8,128)S(1)} %fusion.37), channel_id=2, replica_groups=mesh['seq'=2,'head'=4,'dp'=4] {'seq'}, dimensions={0}, use_global_device_ids=true | all-gather | bytes 786432 | tf_op jit(solution)/shard_map/all_gather | solution.py:11
  44.8 0.8 select_convert_fusion.1
  45.7 1.4 copy-done.2
  47.1 1.8 fusion.36
  48.9 0.2 while.30
  49.0 0.1 add_select_fusion.4
  49.1 1.7 fusion.26
  50.8 3.3 multiply_bitcast_fusion.3
  54.1 0.2 reduce-scatter.10.cloned.1.call-start
  54.3 2.2 fusion.39
  56.6 0.3 fusion.27
  56.9 0.8 copy-done.3
  57.7 3.2 multiply_bitcast_fusion.2
  61.0 3.0 fusion.38
  64.1 1.3 fusion.41
  65.4 0.4 copy-done.19
  65.8 3.3 add_add_fusion
  69.2 2.6 fusion.43
  71.9 0.3 fusion.16
  72.2 1.2 copy-done.17
  73.4 3.2 multiply_bitcast_fusion
  76.7 9.5 %reduce-scatter.12.cloned.1.call-done = f32[256,512]{0,1:T(8,128)} async-done(((f32[2048,512]{0,1:T(8,128)}), f32[256,512]{0,1:T(8,128)}) %reduce-scatter.12.cloned.1.call-update) | async-done | bytes 524304 | tf_op jit(solution)/shard_map/reduce_scatter | solution.py:113
  86.2 2.0 copy.40
  88.2 53.1 %reduce-scatter.8.cloned.1.call-done = f32[256,512]{0,1:T(8,128)} async-done(((f32[2048,512]{0,1:T(8,128)}), f32[256,512]{0,1:T(8,128)}) %reduce-scatter.8.cloned.1.call-update) | async-done | bytes 524304 | tf_op jit(solution)/shard_map/reduce_scatter | solution.py:111
  141.3 2.0 copy.38
  143.3 52.7 %reduce-scatter.10.cloned.1.call-done = f32[256,512]{0,1:T(8,128)} async-done(((f32[2048,512]{0,1:T(8,128)}), f32[256,512]{0,1:T(8,128)}) %reduce-scatter.10.cloned.1.call-update) | async-done | bytes 524304 | tf_op jit(solution)/shard_map/reduce_scatter | solution.py:112
  196.0 2.0 copy.39
  198.0 77.0 %reduce-scatter.6.cloned.1.call-done = f32[512,512]{1,0:T(8,128)} async-done(((f32[512,2048]{1,0:T(8,128)}), f32[512,512]{1,0:T(8,128)}) %reduce-scatter.6.cloned.1.call-update) | async-done | bytes 1048592 | tf_op jit(solution)/shard_map/reduce_scatter | solution.py:92
  275.0 2.1 convert_bitcast_fusion
  277.1 53.6 %reduce-scatter.14.cloned.1.call-done = f32[256,512]{0,1:T(8,128)} async-done(((f32[2048,512]{0,1:T(8,128)}), f32[256,512]{0,1:T(8,128)}) %reduce-scatter.14.cloned.1.call-update) | async-done | bytes 524304 | tf_op jit(solution)/shard_map/reduce_scatter | solution.py:114
  (52 shorter events, 0.5 us)
Async XLA Ops:
  7.2 1.7 copy-start
  7.2 79.0 %reduce-scatter.12.cloned.1.call-start = ((), (), s32[]{:S(2)}) async-start(), calls=%async_computation.8 | async-start | bytes 4718592 | tf_op jit(solution)/shard_map/reduce_scatter | solution.py:113
  8.9 3.0 copy-start.16
  8.9 3.1 copy-start.22
  11.9 15.5 %copy-start.5 = (bf16[512,512]{0,1:T(8,128)(2,1)}, bf16[512,512]{0,1:T(8,128)(2,1)S(1)}, u32[]{:S(2)}) copy-start(bf16[512,512]{0,1:T(8,128)(2,1)S(1)} %fusion.23) | copy-start | bytes 1572868
  13.2 0.8 copy-start.7
  24.4 3.0 copy-start.20
  27.4 8.8 %copy-start.12 = (bf16[512,512]{0,1:T(8,128)(2,1)}, bf16[512,512]{0,1:T(8,128)(2,1)S(1)}, u32[]{:S(2)}) copy-start(bf16[512,512]{0,1:T(8,128)(2,1)S(1)} %fusion.17) | copy-start | bytes 1572868
  27.4 1.2 copy-start.8
  28.6 1.3 copy-start.1
  30.0 3.2 copy-start.14
  33.2 108.1 %reduce-scatter.8.cloned.1.call-start = ((), (), s32[]{:S(2)}) async-start(), calls=%async_computation.6 | async-start | bytes 4718592 | tf_op jit(solution)/shard_map/reduce_scatter | solution.py:111
  36.1 9.5 %copy-start.10 = (bf16[512,512]{0,1:T(8,128)(2,1)}, bf16[512,512]{0,1:T(8,128)(2,1)S(1)}, u32[]{:S(2)}) copy-start(bf16[512,512]{0,1:T(8,128)(2,1)S(1)} %fusion.20) | copy-start | bytes 1572868
  36.2 8.7 %copy-start.9 = (bf16[512,512]{0,1:T(8,128)(2,1)S(1)}, bf16[512,512]{0,1:T(8,128)(2,1)}, u32[]{:S(2)}) copy-start(bf16[512,512]{0,1:T(8,128)(2,1)} %copy-done.7) | copy-start | bytes 1572868
  36.2 8.6 %copy-start.21 = (pred[512,512]{1,0:T(8,128)(4,1)S(1)}, pred[512,512]{1,0:T(8,128)(4,1)}, u32[]{:S(2)}) copy-start(pred[512,512]{1,0:T(8,128)(4,1)} %iota_compare_fusion) | copy-start | bytes 786436
  36.5 10.6 %copy-start.13 = (bf16[512,512]{0,1:T(8,128)(2,1)S(1)}, bf16[512,512]{0,1:T(8,128)(2,1)}, u32[]{:S(2)}) copy-start(bf16[512,512]{0,1:T(8,128)(2,1)} %copy-done.12) | copy-start | bytes 1572868
  45.7 1.4 copy-start.2
  54.1 141.9 %reduce-scatter.10.cloned.1.call-start = ((), (), s32[]{:S(2)}) async-start(), calls=%async_computation.7 | async-start | bytes 4718592 | tf_op jit(solution)/shard_map/reduce_scatter | solution.py:112
  54.3 2.3 copy-start.11
  56.9 0.8 copy-start.3
  60.9 214.1 %reduce-scatter.6.cloned.1.call-start = ((), (), s32[]{:S(2)}) async-start(), calls=%async_computation.5 | async-start | bytes 5242880 | tf_op jit(solution)/shard_map/reduce_scatter | solution.py:92
  61.0 3.1 copy-start.4
  61.0 3.1 copy-start.18
  64.1 1.3 copy-start.15
  64.1 1.8 copy-start.19
  69.2 2.7 copy-start.6
  69.2 261.5 %reduce-scatter.14.cloned.1.call-start = ((), (), s32[]{:S(2)}) async-start(), calls=%async_computation.9 | async-start | bytes 4718592 | tf_op jit(solution)/shard_map/reduce_scatter | solution.py:114
  71.8 1.6 copy-start.17
Sparse Core Ops, SparseCore 0:
  33.3 52.8 reduce-scatter.11
  89.9 51.3 reduce-scatter.7
  144.6 51.3 reduce-scatter.9
  198.2 76.7 reduce-scatter.5
  278.8 51.8 reduce-scatter.13
where the time goes:
time: 338 us; the launch traced here: 337 us
  waiting for transfers between devices  246 us (73%)
  matrix products  42.7 us (13%)
  blocking collectives  18.2 us (5%)
  between operations  14.2 us (4%)
  local copies, waits for them, and re-layouts  12.6 us (4%)
    reduce_scatter x1, waiting for transfers between devices, local(): lax.psum_scatter(head_terms, 'head', scatter_dimension=1, tiled=True)  77 us
    reduce_scatter x1, waiting for transfers between devices, local(): lax.psum_scatter(term_out, ('seq', 'dp'), scatter_dimension=0, tiled=True)  53.6 us
    reduce_scatter x1, waiting for transfers between devices, local(): lax.psum_scatter(term_query, ('seq', 'dp'), scatter_dimension=0, tiled=True)  53.1 us
    reduce_scatter x1, waiting for transfers between devices, local(): lax.psum_scatter(term_key, ('seq', 'dp'), scatter_dimension=0, tiled=True)  52.7 us
    all_gather x2, blocking collectives, entering(): everything = lax.all_gather(x, axis)  18.2 us
    unnamed x49, local copies, waits for them, and re-layouts  12.6 us
    reduce_scatter x1, waiting for transfers between devices, local(): lax.psum_scatter(term_value, ('seq', 'dp'), scatter_dimension=0, tiled=True)  9.51 us
    dot_general x3, matrix products, project(): jnp.dot(in_rows, weight, preferred_element_type=jnp.float32)  8.84 us
  transfers between devices with their start and end apart: 5, of which 5 were waited for; matrix products, arithmetic and copies ran while one was open for 11% of the time, Pallas kernels for 0%

commit v1 on v0

v1 whole, which is shorter than its diff:
```python
import functools

import jax
import jax.numpy as jnp
from jax import lax
from jax.experimental import pallas as pl
from jax.experimental.pallas import tpu as pltpu
from jax.sharding import PartitionSpec as P

HEAD_DIM = 128
BF16 = jnp.bfloat16
F32 = jnp.float32
VMEM_LIMIT = 48 * 1024 * 1024
NN = ((1,), (0,))
NT = ((1,), (1,))
TN = ((0,), (0,))


def dot(a, b, dims):
    return lax.dot_general(a, b, (dims, ((), ())), preferred_element_type=F32)


def shaped(shape, dtype):
    return jax.ShapeDtypeStruct(shape, dtype)


def position_scale(start, rows):
    positions = (start + lax.broadcasted_iota(jnp.int32, (rows, 1), 0)).astype(F32)
    return 1.0 / jnp.sqrt(HEAD_DIM * (positions + 1.0))


def project_kernel(
    seq_ref, x_hbm, o_hbm, wq_hbm, wk_hbm, wv_hbm, wo_hbm,
    q_ref, k_ref, v_ref, g_ref, *rest, one_state,
):
    states, (x_ref, o_ref, wq_ref, wk_ref, wv_ref, wo_ref, sems) = rest[:-7], rest[-7:]
    rows, hd = q_ref.shape
    pairs = (
        (x_hbm, x_ref), (wk_hbm, wk_ref), (wv_hbm, wv_ref),
        (wq_hbm, wq_ref), (o_hbm, o_ref), (wo_hbm, wo_ref),
    )
    copies = [pltpu.make_async_copy(a, b, sems.at[i]) for i, (a, b) in enumerate(pairs)]
    for c in copies[:3]:
        c.start()
    copies[0].wait()
    copies[1].wait()
    for c in copies[3:]:
        c.start()
    k_ref[...] = dot(x_ref[...], wk_ref[...], NN).astype(BF16)
    copies[2].wait()
    v_ref[...] = dot(x_ref[...], wv_ref[...], NN).astype(BF16)
    copies[3].wait()
    q_ref[...] = dot(x_ref[...], wq_ref[...], NN).astype(BF16)
    copies[4].wait()
    copies[5].wait()
    scale = position_scale(seq_ref[0] * rows, rows)
    g_ref[...] = (dot(o_ref[...], wo_ref[...], NT) * scale).astype(BF16)

    def state(a_ref, b_ref, out_ref):
        for h in range(hd // HEAD_DIM):
            at = pl.ds(h * HEAD_DIM, HEAD_DIM)
            out_ref[h] = dot(a_ref[:, at], b_ref[:, at], TN)

    if one_state:

        @pl.when(seq_ref[0] == 0)
        def _():
            state(k_ref, v_ref, states[0])

        @pl.when(seq_ref[0] != 0)
        def _():
            state(q_ref, g_ref, states[0])

    else:
        state(k_ref, v_ref, states[0])
        state(q_ref, g_ref, states[1])


def project(seq_at, in_rows, grad_rows, w_query, w_key, w_value, w_out, one_state):
    rows, width = in_rows.shape
    hd = w_query.shape[1]
    n_states = 1 if one_state else 2
    anywhere = pl.BlockSpec(memory_space=pl.ANY)
    return pl.pallas_call(
        functools.partial(project_kernel, one_state=one_state),
        out_shape=[shaped((rows, hd), BF16)] * 4
        + [shaped((hd // HEAD_DIM, HEAD_DIM, HEAD_DIM), F32)] * n_states,
        in_specs=[pl.BlockSpec(memory_space=pltpu.SMEM)] + [anywhere] * 6,
        out_specs=[pl.BlockSpec(memory_space=pltpu.VMEM)] * (4 + n_states),
        scratch_shapes=[
            pltpu.VMEM((rows, width), BF16),
            pltpu.VMEM((rows, width), BF16),
            pltpu.VMEM((width, hd), BF16),
            pltpu.VMEM((width, hd), BF16),
            pltpu.VMEM((width, hd), BF16),
            pltpu.VMEM((hd, width), BF16),
            pltpu.SemaphoreType.DMA((6,)),
        ],
        compiler_params=pltpu.CompilerParams(vmem_limit_bytes=VMEM_LIMIT),
        cost_estimate=pl.CostEstimate(
            flops=8 * rows * width * hd, bytes_accessed=12 * 2**20, transcendentals=0
        ),
        name="project",
    )(seq_at.reshape(1), in_rows, grad_rows, w_query, w_key, w_value, w_out)


def attend_kernel(
    flags_ref, q_ref, k_ref, v_ref, g_ref, pre_ref, suf_ref,
    first_ref, second_ref, first16_ref, second16_ref,
):
    q, k, v, g = q_ref[...], k_ref[...], v_ref[...], g_ref[...]
    rows = q.shape[0]
    half = rows // 2
    top, low = slice(0, half), slice(half, rows)
    prefix = jnp.where(flags_ref[1] != 0, pre_ref[0], 0.0).astype(BF16)
    suffix = jnp.where(flags_ref[2] != 0, suf_ref[0], 0.0).astype(BF16)

    def causal(a, b):
        r = lax.broadcasted_iota(jnp.int32, (half, half), 0)
        c = lax.broadcasted_iota(jnp.int32, (half, half), 1)
        diagonal = r >= c
        s00 = jnp.where(diagonal, dot(a[top], b[top], NT), 0.0).astype(BF16)
        s10 = dot(a[low], b[top], NT).astype(BF16)
        s11 = jnp.where(diagonal, dot(a[low], b[low], NT), 0.0).astype(BF16)
        return s00, s10, s11

    def forward(s, b):
        s00, s10, s11 = s
        return (dot(s00, b[top], NN), dot(s10, b[top], NN) + dot(s11, b[low], NN))

    def backward(s, a):
        s00, s10, s11 = s
        return (dot(s00, a[top], TN) + dot(s10, a[low], TN), dot(s11, a[low], TN))

    def put(out_ref, out16_ref, at, halves, cross, scale=None):
        for rows_at, inner in zip((top, low), halves):
            value = inner + cross[rows_at]
            if scale is not None:
                value = value * scale[rows_at]
            rounded = value.astype(BF16)
            out16_ref[at, rows_at, :] = rounded
            out_ref[at, rows_at, :] = rounded.astype(F32)

    s_qk = causal(q, k)
    scale = position_scale(flags_ref[0] * rows, rows)
    put(first_ref, first16_ref, 0, forward(s_qk, v), dot(q, prefix, NN), scale)
    put(first_ref, first16_ref, 1, backward(s_qk, g), dot(k, suffix, NN))
    s_gv = causal(g, v)
    put(second_ref, second16_ref, 0, forward(s_gv, k), dot(g, prefix, NT))
    put(second_ref, second16_ref, 1, backward(s_gv, q), dot(v, suffix, NT))


def attend(flags, q, k, v, g, prefix, suffix):
    rows, hd = q.shape
    head = pl.BlockSpec((rows, HEAD_DIM), lambda h: (0, h))
    state = pl.BlockSpec((1, HEAD_DIM, HEAD_DIM), lambda h: (h, 0, 0))
    out = pl.BlockSpec((2, rows, HEAD_DIM), lambda h: (0, 0, h))
    return pl.pallas_call(
        attend_kernel,
        grid=(hd // HEAD_DIM,),
        out_shape=[shaped((2, rows, hd), F32)] * 2 + [shaped((2, rows, hd), BF16)] * 2,
        in_specs=[pl.BlockSpec(memory_space=pltpu.SMEM)] + [head] * 4 + [state] * 2,
        out_specs=[out] * 4,
        compiler_params=pltpu.CompilerParams(vmem_limit_bytes=VMEM_LIMIT),
        cost_estimate=pl.CostEstimate(
            flops=14 * rows * rows * hd, bytes_accessed=8 * 2**20, transcendentals=0
        ),
        name="attend",
    )(flags, q, k, v, g, prefix, suffix)


def head_terms_kernel(d2_ref, d1_ref, wq_ref, wk_ref, wv_ref, out_ref):
    out_ref[...] = (
        dot(d2_ref[0], wq_ref[...], NT)
        + dot(d2_ref[1], wk_ref[...], NT)
        + dot(d1_ref[1], wv_ref[...], NT)
    )


def head_terms(first16, second16, w_query, w_key, w_value):
    width, hd = w_query.shape
    rows = first16.shape[1]
    step = 256
    whole = pl.BlockSpec((2, rows, hd), lambda i: (0, 0, 0))
    weight = pl.BlockSpec((step, hd), lambda i: (i, 0))
    return pl.pallas_call(
        head_terms_kernel,
        grid=(width // step,),
        out_shape=shaped((rows, width), F32),
        in_specs=[whole, whole, weight, weight, weight],
        out_specs=pl.BlockSpec((rows, step), lambda i: (0, i)),
        compiler_params=pltpu.CompilerParams(vmem_limit_bytes=VMEM_LIMIT),
        cost_estimate=pl.CostEstimate(
            flops=6 * rows * width * hd, bytes_accessed=12 * 2**20, transcendentals=0
        ),
        name="head_terms",
    )(second16, first16, w_query, w_key, w_value)


def tiles_kernel(
    at_ref, rows0a, rows0b, rows1a, rows1b, far0a, far0b, far1a, far1b, own_ref, far_ref, *rest,
    out_first, scale, added,
):
    received, outs = (rest[:2], rest[2:]) if added else (None, rest)
    half = own_ref.shape[2] // 2
    inputs = (((rows0a, far0a), (rows0b, far0b)), ((rows1a, far1a), (rows1b, far1b)))
    for side in range(2):
        features = pl.ds(side * half, half)
        for t in range(2):
            near, far = inputs[t][side]
            pair = (
                (near[...], own_ref[t, :, features]),
                (far[...].astype(BF16), far_ref[t, :, features].astype(BF16)),
            )
            if out_first[t]:
                pair = tuple((b, a) for a, b in pair)
            tile = (dot(*pair[0], TN) + dot(*pair[1], TN)) * scale
            if added:
                tile = tile + received[side][0, t]
            outs[side][0, t] = tile


def tiles(near, rows, far, own, other, blocks, out_first, scale, received=None):
    positions, hd = own.shape[1:]
    half = hd // 2
    block = far[0].shape[1] // 4
    low, high = blocks

    def near_spec(which):
        return pl.BlockSpec((positions, block), lambda i, at: (0, at[which[0] + i * (which[1] - which[0])]))

    def far_spec(which):
        return pl.BlockSpec((positions, block), lambda i, at: (0, which[0] + i * (which[1] - which[0])))

    whole = pl.BlockSpec((2, positions, hd), lambda i, at: (0, 0, 0))
    tile = pl.BlockSpec((1, 2, half, block), lambda i, at: (i, 0, 0, 0))
    in_specs = [near_spec(low), near_spec(high)] * 2 + [far_spec(low), far_spec(high)] * 2
    in_specs += [whole, whole]
    args = [rows[0], rows[0], rows[1], rows[1], far[0], far[0], far[1], far[1], own, other]
    if received is not None:
        in_specs += [tile, tile]
        args += list(received)
    return pl.pallas_call(
        functools.partial(
            tiles_kernel, out_first=out_first, scale=scale, added=received is not None
        ),
        grid_spec=pltpu.PrefetchScalarGridSpec(
            num_scalar_prefetch=1, grid=(2,), in_specs=in_specs, out_specs=[tile, tile]
        ),
        out_shape=[shaped((2, 2, half, block), F32)] * 2,
        compiler_params=pltpu.CompilerParams(vmem_limit_bytes=VMEM_LIMIT),
        cost_estimate=pl.CostEstimate(
            flops=8 * 2 * positions * hd * block * 2, bytes_accessed=12 * 2**20, transcendentals=0
        ),
        name="tiles",
    )(near, *args)


def states_before(x, axis, reverse):
    peers, here = (lax.axis_size(axis), lax.axis_index(axis))
    everything = lax.all_gather(x, axis)
    at = jnp.arange(peers)
    reached = at > here if reverse else at < here
    return jnp.sum(jnp.where(reached[:, None, None, None], everything, 0.0), axis=0)


def swap(x, axis, bit):
    return lax.ppermute(x, axis, [(i, i ^ bit) for i in range(lax.axis_size(axis))])


def after(x, done):
    return lax.optimization_barrier((x, done))[0]


def local(layer_input, w_query, w_key, w_value, w_out, out_grad):
    num_rows, width = layer_input.shape[1:]
    hd = w_query.shape[1]
    in_rows = layer_input[0]
    grad_rows = out_grad[0]
    n_seq, n_dp = (lax.axis_size(a) for a in ("seq", "dp"))
    seq_at, dp_at = (lax.axis_index(a) for a in ("seq", "dp"))
    total_rows = n_seq * n_dp * num_rows
    scale = float(total_rows) ** -0.5
    planar = n_seq == 2 and n_dp == 4

    q, k, v, g, *states = project(
        seq_at, in_rows, grad_rows, w_query, w_key, w_value, w_out, n_seq == 2
    )
    if n_seq == 2:
        prefix = suffix = swap(states[0], "seq", 1)
        flags = jnp.stack([seq_at, seq_at, 1 - seq_at]).astype(jnp.int32)
    else:
        prefix = states_before(states[0], "seq", False)
        suffix = states_before(states[1], "seq", True)
        flags = jnp.stack([seq_at, 1, 1]).astype(jnp.int32)

    if planar:
        y_at, core_at = dp_at // 2, dp_at % 2
        block = width // 8
        near = jnp.stack(
            [(seq_at ^ ds) * 4 + (y_at ^ dy) * 2 + core_at for ds in (0, 1) for dy in (0, 1)]
        ).astype(jnp.int32)

        def to_other_core(rows):
            rows = after(rows, states[0])
            parts = [
                lax.dynamic_slice_in_dim(rows, (near[i] ^ 1) * block, block, axis=1)
                for i in range(4)
            ]
            return swap(jnp.concatenate(parts, axis=1).astype(F32), "dp", 1)

        far_in = to_other_core(in_rows)
        far_grad = to_other_core(grad_rows)

    first, second, first16, second16 = attend(flags, q, k, v, g, prefix, suffix)

    if not planar:
        terms = head_terms(first16, second16, w_query, w_key, w_value)
        input_grad = lax.psum_scatter(terms, "head", scatter_dimension=1, tiled=True)

        def reduced(rows, d):
            return lax.psum_scatter(
                dot(rows, d, TN) * scale, ("seq", "dp"), scatter_dimension=0, tiled=True
            )

        return (
            input_grad.astype(BF16)[None],
            reduced(in_rows, second16[0]),
            reduced(in_rows, second16[1]),
            reduced(in_rows, first16[1]),
            reduced(grad_rows, first16[0]).T,
        )

    far_first = swap(first, "dp", 1)
    far_second = swap(second, "dp", 1)
    terms = head_terms(first16, second16, w_query, w_key, w_value)
    input_grad = lax.psum_scatter(terms, "head", scatter_dimension=1, tiled=True)

    def pair(rows, far, own, other, out_first):
        make = functools.partial(tiles, near, rows, far, own, other)
        a, b = make(((2, 3), (1, 3)), out_first, scale)
        a, b = swap(a, "seq", 1), swap(b, "dp", 2)
        a, b = make(((0, 1), (0, 2)), out_first, scale, (a, b))
        return a[0], swap(a[1], "dp", 2), b[0], swap(b[1], "seq", 1)

    a, far_a, b, far_b = pair(
        (grad_rows, in_rows), (far_grad, far_in), first16, far_first, (True, False)
    )
    grad_out = jnp.concatenate([a[0] + far_a[0], b[0] + far_b[0]], axis=0)
    grad_value = jnp.concatenate([a[1] + far_a[1], b[1] + far_b[1]], axis=1)
    a, far_a, b, far_b = pair(
        (in_rows, in_rows), (far_in, far_in), second16, far_second, (False, False)
    )
    grad_query = jnp.concatenate([a[0] + far_a[0], b[0] + far_b[0]], axis=1)
    grad_key = jnp.concatenate([a[1] + far_a[1], b[1] + far_b[1]], axis=1)
    return (input_grad.astype(BF16)[None], grad_query, grad_key, grad_value, grad_out)


def solution(mesh):
    return jax.shard_map(
        local,
        mesh=mesh,
        in_specs=(
            P("dp", "seq", None),
            P(None, "head"),
            P(None, "head"),
            P(None, "head"),
            P("head", None),
            P("dp", "seq", None),
        ),
        out_specs=(
            P("dp", "seq", "head"),
            P(("seq", "dp"), "head"),
            P(("seq", "dp"), "head"),
            P(("seq", "dp"), "head"),
            P("head", ("seq", "dp")),
        ),
        check_vma=False,
    )
```

time: 338 us -> 146 us (0.43)
  waiting for transfers between devices: 246 us -> 58.4 us
  Pallas kernels: 0 us -> 43.2 us
  matrix products: 42.7 us -> 0 us
  blocking collectives: 18.2 us -> 0 us
  starting transfers between devices: 0.39 us -> 11.8 us
  other arithmetic: 3.19 us -> 7.74 us
    reduce_scatter x5 -> x1, waiting for transfers between devices: 246 us -> 0.01 us  [local(): lax.psum_scatter(terms, 'head', scatter_dimension=1, tiled=True)]
    ppermute x0 -> x13, waiting for transfers between devices: none -> 58.4 us  [swap(): lax.ppermute(x, axis, [(i, i ^ bit) for i in range(lax.axis_size(axis))])]
    pallas_call x0 -> x7, Pallas kernels: none -> 43.2 us  [the longest x4 20.5 us: tiles(): pl.pallas_call(functools.partial(tiles_kernel, out_first=out_first, scale...]
    dot_general x23 -> x0, matrix products: 42.7 us -> none  [the longest x3 8.84 us: project(): jnp.dot(in_rows, weight, preferred_element_type=jnp.float32)]
    all_gather x2 -> x0, blocking collectives: 18.2 us -> none  [entering(): everything = lax.all_gather(x, axis)]
    ppermute x0 -> x13, starting transfers between devices: none -> 11.8 us  [swap(): lax.ppermute(x, axis, [(i, i ^ bit) for i in range(lax.axis_size(axis))])]
    unnamed x49 -> x22, local copies, waits for them, and re-layouts: 12.6 us -> 8.44 us
    concatenate x0 -> x4, other arithmetic: none -> 3.42 us  [the longest x1 0.86 us: local(): grad_query = jnp.concatenate([a[0] + far_a[0], b[0] + far_b[0]], axis=1)]
  transfers between devices with their start and end apart: 5 -> 14, of which waited for: 5 -> 11; matrix products, arithmetic and copies ran while one was open for 11% -> 5% of each run, Pallas kernels for 0% -> 14%
where the time goes in v1:
time: 146 us; the launch traced here: 145 us
  waiting for transfers between devices  58.4 us (40%)
  Pallas kernels  43.2 us (30%)
  between operations  14.2 us (10%)
  starting transfers between devices  11.8 us (8%)
  local copies, waits for them, and re-layouts  9.97 us (7%)
  other arithmetic  7.74 us (5%)
    ppermute x13, waiting for transfers between devices, swap(): lax.ppermute(x, axis, [(i, i ^ bit) for i in range(lax.axis_size(axis))])  58.4 us
    pallas_call x4, Pallas kernels, tiles(): pl.pallas_call(functools.partial(tiles_kernel, out_first=out_first, scale...  20.5 us
    ppermute x13, starting transfers between devices, swap(): lax.ppermute(x, axis, [(i, i ^ bit) for i in range(lax.axis_size(axis))])  11.8 us
    pallas_call x1, Pallas kernels, head_terms(): pl.pallas_call(head_terms_kernel, grid=(width // step,), out_shape=shaped...  8.77 us
    unnamed x22, local copies, waits for them, and re-layouts  8.44 us
    pallas_call x1, Pallas kernels, project(): pl.pallas_call(functools.partial(project_kernel, one_state=one_state), ou...  7.16 us
    pallas_call x1, Pallas kernels, attend(): pl.pallas_call(attend_kernel, grid=(hd // HEAD_DIM,), out_shape=[shaped((...  6.76 us
  transfers between devices with their start and end apart: 14, of which 11 were waited for; matrix products, arithmetic and copies ran while one was open for 5% of the time, Pallas kernels for 14%

profile of v1, /device:TPU:0, one launch (start us, length us, event | category | flops | bytes accessed | tf_op | source)
XLA Modules:
  0.0 145.4 jit_solution(16830055897969341160)
XLA Ops:
  7.2 1.6 %copy-done = bf16[1,512,2048]{2,1,0:T(8,128)(2,1)S(1)} copy-done((bf16[1,512,2048]{2,1,0:T(8,128)(2,1)S(1)}, bf16[1,512,2048]{2,1,0:T(8,128)(2,1)}, u32[]{:S(2)}) %copy-start) | copy-done | bytes 2097176
  8.8 7.2 %project.1 = (bf16[512,512]{1,0:T(8,128)(2,1)S(1)}, bf16[512,512]{1,0:T(8,128)(2,1)S(1)}, bf16[512,512]{1,0:T(8,128)(2,1)S(1)}, bf16[512,512]{1,0:T(8,128)(2,1)S(1)}, f32[4,128,128]{2,1,0:T(8,128)S(1)}) custom-call(s32[1]{0:T(128)} %bitcast.seq_ref, bf16[512,2048]{1,0:T(8,128)(2,1)S(1)} %bitcast.74, bf16[512,2048]{1,0:T(8,128)(2,1)} %bitcast.80, ...), custom_call_target="tpu_custom_call" | custom-call | flops 4294967296 | bytes 12582912 | tf_op jit(solution)/shard_map/project/pallas_call | solution.py:84
  16.0 0.8 copy-done.6
  16.8 2.9 %collective-permute-start = (f32[4,128,128]{2,1,0:T(8,128)S(1)}, f32[4,128,128]{2,1,0:T(8,128)S(1)}, u32[]{:S(2)}, u32[]{:S(2)}) collective-permute-start(f32[4,128,128]{2,1,0:T(8,128)S(1)} %get-tuple-element.28), channel_id=1, source_target_pairs={{0,16},{16,0},{1,17},{17,1},{2,18},{18,2},{3,19},{19,3},{4,20},{20... | collective-permute-start | bytes 786440 | tf_op jit(solution)/shard_map/ppermute | solution.py:268
  19.7 0.1 pad_add_fusion.flags_ref
  19.8 6.2 %collective-permute-done.pre_ref.suf_ref = f32[4,128,128]{2,1,0:T(8,128)S(1)} collective-permute-done((f32[4,128,128]{2,1,0:T(8,128)S(1)}, f32[4,128,128]{2,1,0:T(8,128)S(1)}, u32[]{:S(2)}, u32[]{:S(2)}) %collective-permute-start) | collective-permute-done | bytes 262176 | tf_op jit(solution)/shard_map/ppermute | solution.py:268
  26.0 1.0 copy-done.7
  27.1 6.8 %attend.1 = (f32[2,512,512]{2,1,0:T(8,128)}, f32[2,512,512]{2,1,0:T(8,128)}, bf16[2,512,512]{2,1,0:T(8,128)(2,1)S(1)}, bf16[2,512,512]{2,1,0:T(8,128)(2,1)S(1)}) custom-call(s32[3]{0:T(128)S(1)} %pad_add_fusion.flags_ref, bf16[512,512]{1,0:T(8,128)(2,1)S(1)} %get-tuple-element.24.q_ref, bf16[512,512]{1,0:T(8,128)(2,1)S(1)} %get-tuple-element.25.k_ref, ...), custom_call_target="tpu_custom_call" | custom-call | flops 1879048192 | bytes 8388608 | tf_op jit(solution)/shard_map/attend/pallas_call | solution.py:158
  33.8 8.8 %head_terms.1 = f32[512,2048]{1,0:T(8,128)} custom-call(bf16[2,512,512]{2,1,0:T(8,128)(2,1)S(1)} %get-tuple-element.29.d2_ref.own_ref, bf16[2,512,512]{2,1,0:T(8,128)(2,1)S(1)} %get-tuple-element.30.d1_ref.own_ref, bf16[2048,512]{1,0:T(8,128)(2,1)S(1)} %copy-done.5, bf16[2048,512]{1,0:T(8,128)(2,1)} %wk_ref.1, bf16[2048,512]{1,0:T(8,128)(2,1)} %wv_ref.1), custom_call_target="tpu_custom_call" | custom-call | flops 3221225472 | bytes 12582912 | tf_op jit(solution)/shard_map/head_terms/pallas_call | solution.py:186
  42.6 1.0 copy-done.3
  43.6 1.5 %copy-done.1 = bf16[1,512,2048]{2,1,0:T(8,128)(2,1)S(1)} copy-done((bf16[1,512,2048]{2,1,0:T(8,128)(2,1)S(1)}, bf16[1,512,2048]{2,1,0:T(8,128)(2,1)}, u32[]{:S(2)}) %copy-start.1) | copy-done | bytes 2097176
  45.1 1.4 constant_dynamic-slice_fusion.3
  46.6 0.3 maximum_convert_fusion
  46.8 0.1 collective-permute-start.1
  46.9 1.2 copy-done.10
  48.1 1.6 %maximum_convert_fusion.1 = f32[512,1024]{1,0:T(8,128)} fusion(bf16[512,256]{1,0:T(8,128)(2,1)S(1)} %get-tuple-element.44, bf16[512,256]{1,0:T(8,128)(2,1)S(1)} %get-tuple-element.45, bf16[512,256]{1,0:T(8,128)(2,1)S(1)} %get-tuple-element.46, bf16[512,256]{1,0:T(8,128)(2,1)S(1)} %get-tuple-element.43), kind=kLoop, calls=%fused_computation.1 | loop fusion | flops 4194304 | bytes 3145728 | tf_op jit(solution)/shard_map/convert_element_type | solution.py:310
  49.7 0.5 collective-permute-start.7
  50.2 0.1 pad_add_fusion.1.at_ref
  50.3 0.8 collective-permute-done.1.far0a.far0b.far1a.far1b
  51.0 6.0 %collective-permute-done.2.far_ref = f32[2,512,512]{2,1,0:T(8,128)S(1)} collective-permute-done((f32[2,512,512]{2,1,0:T(8,128)S(1)}, f32[2,512,512]{2,1,0:T(8,128)S(1)}, u32[]{:S(2)}, u32[]{:S(2)}) %collective-permute-start.2) | collective-permute-done | bytes 2097184 | tf_op jit(solution)/shard_map/ppermute | solution.py:268
  57.1 1.3 copy-done.9
  58.4 4.7 %tiles.4 = (f32[2,2,256,256]{3,2,1,0:T(8,128)S(1)}, f32[2,2,256,256]{3,2,1,0:T(8,128)S(1)}) custom-call(s32[4]{0:T(128)S(1)} %pad_add_fusion.1.at_ref, bf16[512,2048]{1,0:T(8,128)(2,1)S(1)} %bitcast.76, bf16[512,2048]{1,0:T(8,128)(2,1)S(1)} %bitcast.77, bf16[512,2048]{1,0:T(8,128)(2,1)S(1)} %bitcast.78, bf16[512,2048]{1,0:T(8,128)(2,1)S(1)} %bitcast.79, ...), custom_call_target="tpu_custom_call" | custom-call | flops 2147483648 | bytes 12582912 | tf_op jit(solution)/shard_map/tiles/pallas_call | solution.py:243
  63.1 1.8 %collective-permute-start.3 = (f32[2,2,256,256]{3,2,1,0:T(8,128)S(1)}, f32[2,2,256,256]{3,2,1,0:T(8,128)S(1)}, u32[]{:S(2)}, u32[]{:S(2)}) collective-permute-start(f32[2,2,256,256]{3,2,1,0:T(8,128)S(1)} %get-tuple-element.33), channel_id=1, source_target_pairs={{0,16},{16,0},{1,17},{17,1},{2,18},{18,2},{3,19},{19,3},{4,20},{20... | collective-permute-start | bytes 3145736 | tf_op jit(solution)/shard_map/ppermute | solution.py:268
  64.9 1.5 %collective-permute-start.4 = (f32[2,2,256,256]{3,2,1,0:T(8,128)S(1)}, f32[2,2,256,256]{3,2,1,0:T(8,128)S(1)}, u32[]{:S(2)}, u32[]{:S(2)}) collective-permute-start(f32[2,2,256,256]{3,2,1,0:T(8,128)S(1)} %get-tuple-element.34), channel_id=1, source_target_pairs={{0,2},{1,3},{2,0},{3,1},{4,6},{5,7},{6,4},{7,5},{8,10},{9,11},{10,... | collective-permute-start | bytes 3145736 | tf_op jit(solution)/shard_map/ppermute | solution.py:268
  66.4 4.8 %tiles.6 = (f32[2,2,256,256]{3,2,1,0:T(8,128)S(1)}, f32[2,2,256,256]{3,2,1,0:T(8,128)S(1)}) custom-call(s32[4]{0:T(128)S(1)} %pad_add_fusion.1.at_ref, bf16[512,2048]{1,0:T(8,128)(2,1)S(1)} %bitcast.84, bf16[512,2048]{1,0:T(8,128)(2,1)S(1)} %bitcast.85, bf16[512,2048]{1,0:T(8,128)(2,1)} %bitcast.66, bf16[512,2048]{1,0:T(8,128)(2,1)} %bitcast.67, ...), custom_call_target="tpu_custom_call" | custom-call | flops 2147483648 | bytes 12582912 | tf_op jit(solution)/shard_map/tiles/pallas_call | solution.py:243
  71.2 0.5 collective-permute-start.9
  71.8 0.3 collective-permute-start.10
  72.1 17.0 %collective-permute-done.3.rest_0_ = f32[2,2,256,256]{3,2,1,0:T(8,128)S(1)} collective-permute-done((f32[2,2,256,256]{3,2,1,0:T(8,128)S(1)}, f32[2,2,256,256]{3,2,1,0:T(8,128)S(1)}, u32[]{:S(2)}, u32[]{:S(2)}) %collective-permute-start.3) | collective-permute-done | bytes 1048608 | tf_op jit(solution)/shard_map/ppermute | solution.py:268
  89.1 1.8 %collective-permute-done.4.rest_1_ = f32[2,2,256,256]{3,2,1,0:T(8,128)S(1)} collective-permute-done((f32[2,2,256,256]{3,2,1,0:T(8,128)S(1)}, f32[2,2,256,256]{3,2,1,0:T(8,128)S(1)}, u32[]{:S(2)}, u32[]{:S(2)}) %collective-permute-start.4) | collective-permute-done | bytes 1048608 | tf_op jit(solution)/shard_map/ppermute | solution.py:268
  90.9 5.7 %tiles.5 = (f32[2,2,256,256]{3,2,1,0:T(8,128)S(1)}, f32[2,2,256,256]{3,2,1,0:T(8,128)S(1)}) custom-call(s32[4]{0:T(128)S(1)} %pad_add_fusion.1.at_ref, bf16[512,2048]{1,0:T(8,128)(2,1)} %bitcast.68, bf16[512,2048]{1,0:T(8,128)(2,1)} %bitcast.69, bf16[512,2048]{1,0:T(8,128)(2,1)} %bitcast.70, bf16[512,2048]{1,0:T(8,128)(2,1)} %bitcast.71, ...), custom_call_target="tpu_custom_call" | custom-call | flops 2147483648 | bytes 12582912 | tf_op jit(solution)/shard_map/tiles/pallas_call | solution.py:243
  96.6 0.5 collective-permute-start.6
  97.1 1.5 %collective-permute-start.5 = (f32[2,256,256]{2,1,0:T(8,128)S(1)}, f32[2,256,256]{2,1,0:T(8,128)S(1)}, u32[]{:S(2)}, u32[]{:S(2)}) collective-permute-start(f32[2,256,256]{2,1,0:T(8,128)S(1)} %slice_bitcast_fusion.3), channel_id=1, source_target_pairs={{0,2},{1,3},{2,0},{3,1},{4,6},{5,7},{6,4},{7,5},{8,10},{9,11},{10,... | collective-permute-start | bytes 1572872 | tf_op jit(solution)/shard_map/ppermute | solution.py:268
  98.6 13.0 %collective-permute-done.9.rest_0_ = f32[2,2,256,256]{3,2,1,0:T(8,128)S(1)} collective-permute-done((f32[2,2,256,256]{3,2,1,0:T(8,128)S(1)}, f32[2,2,256,256]{3,2,1,0:T(8,128)S(1)}, u32[]{:S(2)}, u32[]{:S(2)}) %collective-permute-start.9) | collective-permute-done | bytes 1048608 | tf_op jit(solution)/shard_map/ppermute | solution.py:268
  111.6 1.8 %collective-permute-done.10.rest_1_ = f32[2,2,256,256]{3,2,1,0:T(8,128)S(1)} collective-permute-done((f32[2,2,256,256]{3,2,1,0:T(8,128)S(1)}, f32[2,2,256,256]{3,2,1,0:T(8,128)S(1)}, u32[]{:S(2)}, u32[]{:S(2)}) %collective-permute-start.10) | collective-permute-done | bytes 1048608 | tf_op jit(solution)/shard_map/ppermute | solution.py:268
  113.4 5.4 %tiles.7 = (f32[2,2,256,256]{3,2,1,0:T(8,128)S(1)}, f32[2,2,256,256]{3,2,1,0:T(8,128)S(1)}) custom-call(s32[4]{0:T(128)S(1)} %pad_add_fusion.1.at_ref, bf16[512,2048]{1,0:T(8,128)(2,1)} %bitcast.82, bf16[512,2048]{1,0:T(8,128)(2,1)} %bitcast.83, bf16[512,2048]{1,0:T(8,128)(2,1)} %bitcast.72, bf16[512,2048]{1,0:T(8,128)(2,1)} %bitcast.73, ...), custom_call_target="tpu_custom_call" | custom-call | flops 2147483648 | bytes 12582912 | tf_op jit(solution)/shard_map/tiles/pallas_call | solution.py:243
  118.8 0.3 collective-permute-start.12
  119.2 1.8 %collective-permute-start.11 = (f32[2,256,256]{2,1,0:T(8,128)S(1)}, f32[2,256,256]{2,1,0:T(8,128)S(1)}, u32[]{:S(2)}, u32[]{:S(2)}) collective-permute-start(f32[2,256,256]{2,1,0:T(8,128)S(1)} %slice_bitcast_fusion.1), channel_id=1, source_target_pairs={{0,2},{1,3},{2,0},{3,1},{4,6},{5,7},{6,4},{7,5},{8,10},{9,11},{10,... | collective-permute-start | bytes 1572872 | tf_op jit(solution)/shard_map/ppermute | solution.py:268
  120.9 1.9 %collective-permute-done.6 = f32[2,256,256]{2,1,0:T(8,128)S(1)} collective-permute-done((f32[2,256,256]{2,1,0:T(8,128)S(1)}, f32[2,256,256]{2,1,0:T(8,128)S(1)}, u32[]{:S(2)}, u32[]{:S(2)}) %collective-permute-start.6) | collective-permute-done | bytes 524320 | tf_op jit(solution)/shard_map/ppermute | solution.py:268
  122.8 0.1 fusion.4
  122.9 1.7 %collective-permute-done.5 = f32[2,256,256]{2,1,0:T(8,128)S(1)} collective-permute-done((f32[2,256,256]{2,1,0:T(8,128)S(1)}, f32[2,256,256]{2,1,0:T(8,128)S(1)}, u32[]{:S(2)}, u32[]{:S(2)}) %collective-permute-start.5) | collective-permute-done | bytes 524320 | tf_op jit(solution)/shard_map/ppermute | solution.py:268
  124.7 0.9 pad_maximum_fusion
  125.6 0.9 pad_maximum_fusion.1
  126.4 6.8 %collective-permute-done.12 = f32[2,256,256]{2,1,0:T(8,128)S(1)} collective-permute-done((f32[2,256,256]{2,1,0:T(8,128)S(1)}, f32[2,256,256]{2,1,0:T(8,128)S(1)}, u32[]{:S(2)}, u32[]{:S(2)}) %collective-permute-start.12) | collective-permute-done | bytes 524320 | tf_op jit(solution)/shard_map/ppermute | solution.py:268
  133.3 1.4 collective-permute-done.11
  134.7 0.1 fusion.1
  134.8 0.9 pad_maximum_fusion.2
  135.6 0.8 pad_maximum_fusion.3
  136.5 2.1 %convert_bitcast_fusion = bf16[1,512,512]{2,1,0:T(8,128)(2,1)} fusion(f32[512,512]{1,0:T(8,128)} %reduce-scatter.2.cloned.1.call-done), kind=kLoop, calls=%fused_computation.10 | loop fusion | flops 262144 | bytes 1572864 | tf_op jit(solution)/shard_map/broadcast_in_dim | solution.py:356
  (28 shorter events, 0.4 us)
Async XLA Ops:
  7.2 129.3 %reduce-scatter.2.cloned.1.call-start = ((), (), s32[]{:S(2)}) async-start(), calls=%async_computation.1 | async-start | bytes 5242880 | tf_op jit(solution)/shard_map/reduce_scatter | solution.py:337
  7.2 1.6 %copy-start = (bf16[1,512,2048]{2,1,0:T(8,128)(2,1)S(1)}, bf16[1,512,2048]{2,1,0:T(8,128)(2,1)}, u32[]{:S(2)}) copy-start(bf16[1,512,2048]{2,1,0:T(8,128)(2,1)} %param.6) | copy-start | bytes 6291460
  16.0 0.8 copy-start.6
  16.8 9.2 %collective-permute-start = (f32[4,128,128]{2,1,0:T(8,128)S(1)}, f32[4,128,128]{2,1,0:T(8,128)S(1)}, u32[]{:S(2)}, u32[]{:S(2)}) collective-permute-start(f32[4,128,128]{2,1,0:T(8,128)S(1)} %get-tuple-element.28), channel_id=1, source_target_pairs={{0,16},{16,0},{1,17},{17,1},{2,18},{18,2},{3,19},{19,3},{4,20},{20... | collective-permute-start | bytes 786440 | tf_op jit(solution)/shard_map/ppermute | solution.py:268
  26.0 1.0 copy-start.7
  27.1 6.8 %copy-start.5 = (bf16[2048,512]{1,0:T(8,128)(2,1)S(1)}, bf16[2048,512]{1,0:T(8,128)(2,1)}, u32[]{:S(2)}) copy-start(bf16[2048,512]{1,0:T(8,128)(2,1)} %wq_ref.1) | copy-start | bytes 6291460
  42.6 1.0 copy-start.3
  43.6 1.6 %copy-start.1 = (bf16[1,512,2048]{2,1,0:T(8,128)(2,1)S(1)}, bf16[1,512,2048]{2,1,0:T(8,128)(2,1)}, u32[]{:S(2)}) copy-start(bf16[1,512,2048]{2,1,0:T(8,128)(2,1)} %param.6) | copy-start | bytes 6291460
  46.5 1.6 %copy-start.10 = (f32[2,512,512]{2,1,0:T(8,128)S(1)}, f32[2,512,512]{2,1,0:T(8,128)}, u32[]{:S(2)}) copy-start(f32[2,512,512]{2,1,0:T(8,128)} %get-tuple-element.32) | copy-start | bytes 6291460
  46.8 11.5 %copy-start.4 = (bf16[2,512,512]{2,1,0:T(8,128)(2,1)S(1)}, bf16[2,512,512]{2,1,0:T(8,128)(2,1)}, u32[]{:S(2)}) copy-start(bf16[2,512,512]{2,1,0:T(8,128)(2,1)} %copy-done.3) | copy-start | bytes 3145732
  46.8 4.2 %collective-permute-start.1 = (f32[512,1024]{1,0:T(8,128)S(1)}, f32[512,1024]{1,0:T(8,128)S(1)}, u32[]{:S(2)}, u32[]{:S(2)}) collective-permute-start(f32[512,1024]{1,0:T(8,128)S(1)} %maximum_convert_fusion), channel_id=1, source_target_pairs={{0,1},{1,0},{2,3},{3,2},{4,5},{5,4},{6,7},{7,6},{8,9},{9,8},{10,11... | collective-permute-start | bytes 6291464 | tf_op jit(solution)/shard_map/ppermute | solution.py:268
  48.1 8.9 %collective-permute-start.2 = (f32[2,512,512]{2,1,0:T(8,128)S(1)}, f32[2,512,512]{2,1,0:T(8,128)S(1)}, u32[]{:S(2)}, u32[]{:S(2)}) collective-permute-start(f32[2,512,512]{2,1,0:T(8,128)S(1)} %copy-done.10), channel_id=1, source_target_pairs={{0,1},{1,0},{2,3},{3,2},{4,5},{5,4},{6,7},{7,6},{8,9},{9,8},{10,11... | collective-permute-start | bytes 6291464 | tf_op jit(solution)/shard_map/ppermute | solution.py:268
  49.7 16.7 %collective-permute-start.7 = (f32[512,1024]{1,0:T(8,128)}, f32[512,1024]{1,0:T(8,128)}, u32[]{:S(2)}, u32[]{:S(2)}) collective-permute-start(f32[512,1024]{1,0:T(8,128)} %maximum_convert_fusion.1), channel_id=1, source_target_pairs={{0,1},{1,0},{2,3},{3,2},{4,5},{5,4},{6,7},{7,6},{8,9},{9,8},{10,11... | collective-permute-start | bytes 6291464 | tf_op jit(solution)/shard_map/ppermute | solution.py:268
  50.2 16.2 %collective-permute-start.8 = (f32[2,512,512]{2,1,0:T(8,128)}, f32[2,512,512]{2,1,0:T(8,128)}, u32[]{:S(2)}, u32[]{:S(2)}) collective-permute-start(f32[2,512,512]{2,1,0:T(8,128)} %get-tuple-element.38), channel_id=1, source_target_pairs={{0,1},{1,0},{2,3},{3,2},{4,5},{5,4},{6,7},{7,6},{8,9},{9,8},{10,11... | collective-permute-start | bytes 6291464 | tf_op jit(solution)/shard_map/ppermute | solution.py:268
  50.3 16.1 %copy-start.2 = (bf16[1,512,2048]{2,1,0:T(8,128)(2,1)S(1)}, bf16[1,512,2048]{2,1,0:T(8,128)(2,1)}, u32[]{:S(2)}) copy-start(bf16[1,512,2048]{2,1,0:T(8,128)(2,1)} %param.11) | copy-start | bytes 6291460
  51.0 6.0 %copy-start.8 = (f32[512,1024]{1,0:T(8,128)}, f32[512,1024]{1,0:T(8,128)S(1)}, u32[]{:S(2)}) copy-start(f32[512,1024]{1,0:T(8,128)S(1)} %collective-permute-done.1.far0a.far0b.far1a.far1b) | copy-start | bytes 6291460
  57.0 1.3 copy-start.9
  63.1 26.1 %collective-permute-start.3 = (f32[2,2,256,256]{3,2,1,0:T(8,128)S(1)}, f32[2,2,256,256]{3,2,1,0:T(8,128)S(1)}, u32[]{:S(2)}, u32[]{:S(2)}) collective-permute-start(f32[2,2,256,256]{3,2,1,0:T(8,128)S(1)} %get-tuple-element.33), channel_id=1, source_target_pairs={{0,16},{16,0},{1,17},{17,1},{2,18},{18,2},{3,19},{19,3},{4,20},{20... | collective-permute-start | bytes 3145736 | tf_op jit(solution)/shard_map/ppermute | solution.py:268
  64.9 26.0 %collective-permute-start.4 = (f32[2,2,256,256]{3,2,1,0:T(8,128)S(1)}, f32[2,2,256,256]{3,2,1,0:T(8,128)S(1)}, u32[]{:S(2)}, u32[]{:S(2)}) collective-permute-start(f32[2,2,256,256]{3,2,1,0:T(8,128)S(1)} %get-tuple-element.34), channel_id=1, source_target_pairs={{0,2},{1,3},{2,0},{3,1},{4,6},{5,7},{6,4},{7,5},{8,10},{9,11},{10,... | collective-permute-start | bytes 3145736 | tf_op jit(solution)/shard_map/ppermute | solution.py:268
  71.2 40.4 %collective-permute-start.9 = (f32[2,2,256,256]{3,2,1,0:T(8,128)S(1)}, f32[2,2,256,256]{3,2,1,0:T(8,128)S(1)}, u32[]{:S(2)}, u32[]{:S(2)}) collective-permute-start(f32[2,2,256,256]{3,2,1,0:T(8,128)S(1)} %get-tuple-element.39), channel_id=1, source_target_pairs={{0,16},{16,0},{1,17},{17,1},{2,18},{18,2},{3,19},{19,3},{4,20},{20... | collective-permute-start | bytes 3145736 | tf_op jit(solution)/shard_map/ppermute | solution.py:268
  71.8 41.6 %collective-permute-start.10 = (f32[2,2,256,256]{3,2,1,0:T(8,128)S(1)}, f32[2,2,256,256]{3,2,1,0:T(8,128)S(1)}, u32[]{:S(2)}, u32[]{:S(2)}) collective-permute-start(f32[2,2,256,256]{3,2,1,0:T(8,128)S(1)} %get-tuple-element.40), channel_id=1, source_target_pairs={{0,2},{1,3},{2,0},{3,1},{4,6},{5,7},{6,4},{7,5},{8,10},{9,11},{10,... | collective-permute-start | bytes 3145736 | tf_op jit(solution)/shard_map/ppermute | solution.py:268
  96.6 26.2 %collective-permute-start.6 = (f32[2,256,256]{2,1,0:T(8,128)S(1)}, f32[2,256,256]{2,1,0:T(8,128)S(1)}, u32[]{:S(2)}, u32[]{:S(2)}) collective-permute-start(f32[2,256,256]{2,1,0:T(8,128)S(1)} %slice_bitcast_fusion.2), channel_id=1, source_target_pairs={{0,16},{16,0},{1,17},{17,1},{2,18},{18,2},{3,19},{19,3},{4,20},{20... | collective-permute-start | bytes 1572872 | tf_op jit(solution)/shard_map/ppermute | solution.py:268
  97.1 27.5 %collective-permute-start.5 = (f32[2,256,256]{2,1,0:T(8,128)S(1)}, f32[2,256,256]{2,1,0:T(8,128)S(1)}, u32[]{:S(2)}, u32[]{:S(2)}) collective-permute-start(f32[2,256,256]{2,1,0:T(8,128)S(1)} %slice_bitcast_fusion.3), channel_id=1, source_target_pairs={{0,2},{1,3},{2,0},{3,1},{4,6},{5,7},{6,4},{7,5},{8,10},{9,11},{10,... | collective-permute-start | bytes 1572872 | tf_op jit(solution)/shard_map/ppermute | solution.py:268
  118.8 14.5 %collective-permute-start.12 = (f32[2,256,256]{2,1,0:T(8,128)S(1)}, f32[2,256,256]{2,1,0:T(8,128)S(1)}, u32[]{:S(2)}, u32[]{:S(2)}) collective-permute-start(f32[2,256,256]{2,1,0:T(8,128)S(1)} %slice_bitcast_fusion), channel_id=1, source_target_pairs={{0,16},{16,0},{1,17},{17,1},{2,18},{18,2},{3,19},{19,3},{4,20},{20... | collective-permute-start | bytes 1572872 | tf_op jit(solution)/shard_map/ppermute | solution.py:268
  119.2 15.6 %collective-permute-start.11 = (f32[2,256,256]{2,1,0:T(8,128)S(1)}, f32[2,256,256]{2,1,0:T(8,128)S(1)}, u32[]{:S(2)}, u32[]{:S(2)}) collective-permute-start(f32[2,256,256]{2,1,0:T(8,128)S(1)} %slice_bitcast_fusion.1), channel_id=1, source_target_pairs={{0,2},{1,3},{2,0},{3,1},{4,6},{5,7},{6,4},{7,5},{8,10},{9,11},{10,... | collective-permute-start | bytes 1572872 | tf_op jit(solution)/shard_map/ppermute | solution.py:268
Sparse Core Ops, SparseCore 0:
  43.7 78.2 reduce-scatter.1
